TPU v7x, 32 devices: a whole 2x2x4 slice. The times are simulated.
32 devices in a mesh: dp: 4 (over y, core), mp: 8 (over z, x).
Axes of the slice: x: 2, y: 2, z: 4, core: 2. Of those that a mesh axis runs over, the one named last changes fastest.
Arguments:
- tokens: bfloat16 [4096, 2048], P(('dp', 'mp')), may hold values from -6 to 6
- norm_gain: float32 [2048], replicated, may hold values from 0.1 to 1.9
- router: bfloat16 [2048, 8], replicated, may hold values from -0.125 to 0.125
- routes: int32 [4096, 2], P(('dp', 'mp')), may hold values from 0 to 7, all different within a row; in each aligned block of 128 rows (0 to 127, 128 to 255, ...) at most 40 rows name the same one
- prompt_lengths: int32 [8], replicated, may hold values from 256 to 512, as said below
- wq_train: float32 [8, 2048, 2048], P(None, ('dp', 'mp'))
- wo_train: float32 [8, 2048, 2048], P(None, ('dp', 'mp')), may hold values from -0.25 to 0.25
- wkv_train: float32 [2048, 4096], P(('dp', 'mp'))
- page_table: int32 [4, 8, 8], P('dp', 'mp'), may hold values from 0 to 127, as said below
Outputs:
- attn_out: bfloat16 [4096, 2048], P(('dp', 'mp'))
- kv_pool: bfloat16 [512, 16, 4096], P(('dp', 'mp'))
Inputs may be any that keep to these rules, and one draw needn't show every extreme that they name: `routes`: each of the two entries of a row names a different expert; in the rows of one device (aligned blocks of 128 rows) no expert is named by more than 40 rows, a bound that some block reaches. `prompt_lengths`: every prompt uses at least 256 slots; some prompt uses all 512 and another exactly 256. `page_table`: entry [g, w, q] equals owner * 16 + w * 2 + c with c < 2; the pairs (owner, c) of one writer w in one group are distinct, so at most 2 pages of one writer go to one owner. In every group one owner receives 2 pages from every writer. Pool pages that no entry names stay zero.
All inputs are finite; a program needn't handle non-finite values.
Results may differ from a plain program's by a relative error of at most 0.012.
The roundings to bfloat16 on the way count: a program that leaves them out, or rounds other values in their place, can miss the bound.
Values may be sent and summed in bfloat16 or wider, within the bound.
A program may use at most 192 MiB of HBM per device.

v0:
```python
import jax
import jax.numpy as jnp
from jax import lax
from jax.sharding import PartitionSpec as P

HD = 128
PAGE = 16
PCAP = 2


def rotate(vectors, positions):
    half_dim = vectors.shape[-1] // 2
    frequency = 10000.0 ** (-(jnp.arange(half_dim, dtype=jnp.float32) * 2.0 / vectors.shape[-1]))
    angles = positions.astype(jnp.float32)[:, None] * frequency[None, :]
    cosine = jnp.cos(angles)[:, None, :]
    sine = jnp.sin(angles)[:, None, :]
    leading = vectors[..., :half_dim]
    trailing = vectors[..., half_dim:]
    return jnp.concatenate(
        [leading * cosine - trailing * sine, trailing * cosine + leading * sine], axis=-1
    )


def on_device(
    tokens, norm_gain, router, routes, prompt_lengths, wq_train, wo_train, wkv_train, page_table
):
    mp_count = lax.axis_size("mp")
    experts = wq_train.shape[0]
    blocks = mp_count // experts
    width = wq_train.shape[2]
    block_width = width // blocks
    head_dim = HD
    block_heads = block_width // head_dim
    tok_rows = tokens.shape[0]
    model_width = tokens.shape[1]
    capacity = tok_rows // 4 + tok_rows // 16
    prompt_len = tok_rows * mp_count // 2
    writer_pages = tok_rows * blocks // PAGE
    slot_count = mp_count * PCAP
    device = lax.axis_index("mp")
    expert = device // blocks
    prompt_group = lax.axis_index("dp")
    shard_rows = wq_train.shape[1]
    query_part = wq_train.reshape(experts, shard_rows, blocks, block_width).transpose(0, 2, 1, 3)
    query_part = query_part.reshape(mp_count, shard_rows, block_width).astype(jnp.bfloat16)
    output_part = wo_train.reshape(experts, shard_rows, blocks, block_width).transpose(0, 2, 1, 3)
    output_part = output_part.reshape(mp_count, shard_rows, block_width).astype(jnp.bfloat16)
    pair_part = wkv_train.reshape(shard_rows, 2, blocks, block_width).transpose(2, 0, 1, 3)
    pair_part = pair_part.reshape(blocks, shard_rows, 2 * block_width)
    pair_part = jnp.broadcast_to(pair_part[None], (experts, blocks, shard_rows, 2 * block_width))
    pair_part = pair_part.reshape(mp_count, shard_rows, 2 * block_width).astype(jnp.bfloat16)
    exchanged = (
        lax.all_to_all(query_part, "mp", split_axis=0, concat_axis=1, tiled=True),
        lax.all_to_all(output_part, "mp", split_axis=0, concat_axis=1, tiled=True),
        lax.all_to_all(pair_part, "mp", split_axis=0, concat_axis=1, tiled=True),
    )
    query_w, output_w, pair_w = (
        lax.all_gather(exchanged[0], "dp", axis=1, tiled=True),
        lax.all_gather(exchanged[1], "dp", axis=1, tiled=True),
        lax.all_gather(exchanged[2], "dp", axis=1, tiled=True),
    )
    query_w = query_w[0]
    output_w = output_w[0]
    pair_w = pair_w[0]
    wide_tokens = tokens.astype(jnp.float32)
    normed = (
        wide_tokens
        * lax.rsqrt(jnp.mean(wide_tokens * wide_tokens, axis=-1, keepdims=True) + 1e-06)
        * norm_gain
    ).astype(jnp.bfloat16)
    logits = jnp.dot(normed, router, preferred_element_type=jnp.float32)
    labels = jnp.arange(experts, dtype=jnp.int32)
    first_hot = routes[:, 0][None, :] == labels[:, None]
    second_hot = routes[:, 1][None, :] == labels[:, None]
    first_logit = jnp.sum(jnp.where(first_hot.T, logits, 0.0), axis=1)
    second_logit = jnp.sum(jnp.where(second_hot.T, logits, 0.0), axis=1)
    gate_first = 1.0 / (1.0 + jnp.exp(second_logit - first_logit))
    gate_second = 1.0 / (1.0 + jnp.exp(first_logit - second_logit))
    gates = jnp.where(
        first_hot, gate_first[None, :], jnp.where(second_hot, gate_second[None, :], 0.0)
    )
    named = first_hot | second_hot
    ranking = jnp.cumsum(named.astype(jnp.int32), axis=1) - 1
    chosen = named[:, None, :] & (
        ranking[:, None, :] == jnp.arange(capacity, dtype=jnp.int32)[None, :, None]
    )
    slot_row = jnp.sum(
        jnp.where(chosen, jnp.arange(tok_rows, dtype=jnp.int32)[None, None, :], 0), axis=-1
    )
    filled = jnp.any(chosen, axis=-1)
    picked = jnp.where(filled[..., None], normed[slot_row], jnp.zeros((), jnp.bfloat16))
    outgoing = jnp.broadcast_to(picked[:, None], (experts, blocks, capacity, model_width)).reshape(
        mp_count, capacity, model_width
    )
    places = jnp.where(filled, (device * tok_rows + slot_row) % prompt_len, 0)
    outgoing_places = jnp.broadcast_to(places[:, None], (experts, blocks, capacity)).reshape(
        mp_count, capacity
    )
    arrived = lax.all_to_all(outgoing, "mp", split_axis=0, concat_axis=0, tiled=True)
    arrived_places = lax.all_to_all(outgoing_places, "mp", split_axis=0, concat_axis=0, tiled=True)
    segment = lax.all_gather(normed, "mp", axis=0, tiled=True)
    projected = jnp.dot(segment, pair_w, preferred_element_type=jnp.float32)
    row_places = jnp.arange(segment.shape[0], dtype=jnp.int32) % prompt_len
    keyed = rotate(
        projected[:, :block_width].reshape(-1, block_heads, head_dim), row_places
    ).reshape(-1, block_width)
    kv_rows = jnp.concatenate([keyed, projected[:, block_width:]], axis=1).astype(jnp.bfloat16)
    own_pages = lax.dynamic_slice_in_dim(
        kv_rows, expert * writer_pages * PAGE, writer_pages * PAGE, 0
    )
    own_pages = own_pages.reshape(writer_pages, PAGE, 2 * block_width)
    page_ids = page_table[0, 0]
    target_cells = page_ids // slot_count * PCAP + page_ids % PCAP
    placing = (
        target_cells[None, :] == jnp.arange(mp_count * PCAP, dtype=jnp.int32)[:, None]
    ).astype(jnp.bfloat16)
    outgoing_pages = jnp.einsum(
        "cq,qpk->cpk", placing, own_pages, preferred_element_type=jnp.float32
    ).astype(jnp.bfloat16)
    outgoing_pages = outgoing_pages.reshape(mp_count, PCAP, PAGE, 2 * block_width)
    page_pool = lax.all_to_all(outgoing_pages, "mp", split_axis=0, concat_axis=0, tiled=True)
    queries = jnp.dot(arrived.reshape(-1, model_width), query_w, preferred_element_type=jnp.float32)
    query_places = arrived_places.reshape(-1)
    queries = (
        rotate(queries.reshape(-1, block_heads, head_dim), query_places) * head_dim ** (-0.5)
    ).astype(jnp.bfloat16)
    key_side = (
        kv_rows[:, :block_width].reshape(2, prompt_len, block_heads, head_dim).transpose(0, 2, 1, 3)
    )
    value_side = (
        kv_rows[:, block_width:].reshape(2, prompt_len, block_heads, head_dim).transpose(0, 2, 1, 3)
    )
    key_index = jnp.arange(prompt_len, dtype=jnp.int32)
    half_rows = mp_count // 2 * capacity
    sides = []
    for side in range(2):
        side_places = query_places[side * half_rows : (side + 1) * half_rows]
        length = prompt_lengths[2 * prompt_group + side]
        allowed = (key_index[None, :] <= side_places[:, None]) & (key_index[None, :] < length)
        side_queries = queries[side * half_rows : (side + 1) * half_rows].transpose(1, 0, 2)

        def one_head(operands):
            query_head, key_head, value_head = operands
            scores = lax.dot_general(
                query_head, key_head, (((1,), (1,)), ((), ())), preferred_element_type=jnp.float32
            )
            scores = jnp.where(allowed, scores, -jnp.inf)
            highest = jnp.max(scores, axis=-1, keepdims=True)
            powered = jnp.exp(scores - highest)
            softened = (powered / jnp.sum(powered, axis=-1, keepdims=True)).astype(jnp.bfloat16)
            return jnp.dot(softened, value_head, preferred_element_type=jnp.float32).astype(
                jnp.bfloat16
            )

        sides.append(lax.map(one_head, (side_queries, key_side[side], value_side[side])))
    heads_out = jnp.stack(sides).transpose(0, 2, 1, 3).reshape(2 * half_rows, block_width)
    partial_value = lax.dot_general(
        heads_out, output_w, (((1,), (1,)), ((), ())), preferred_element_type=jnp.float32
    )
    partial_value = partial_value.astype(jnp.bfloat16).reshape(mp_count, capacity, model_width)
    returned = lax.all_to_all(partial_value, "mp", split_axis=0, concat_axis=0, tiled=True)
    page_pool = page_pool.reshape(slot_count, PAGE, 2 * block_width)
    summed = (
        returned.astype(jnp.float32).reshape(experts, blocks, capacity, model_width).sum(axis=1)
    )
    summed = summed.reshape(experts * capacity, model_width)
    weights = jnp.where(chosen, gates[:, None, :], 0.0).reshape(experts * capacity, tok_rows)
    mixed = lax.dot_general(
        weights,
        summed,
        (((0,), (0,)), ((), ())),
        precision=lax.Precision.HIGHEST,
        preferred_element_type=jnp.float32,
    )
    return (mixed.astype(jnp.bfloat16), page_pool)


def solution(mesh):
    placed = (
        P(("dp", "mp"), None),
        P(),
        P(),
        P(("dp", "mp"), None),
        P(),
        P(None, ("dp", "mp"), None),
        P(None, ("dp", "mp"), None),
        P(("dp", "mp"), None),
        P("dp", "mp", None),
    )
    return jax.shard_map(
        on_device,
        mesh=mesh,
        in_specs=placed,
        out_specs=(P(("dp", "mp"), None), P(("dp", "mp"), None, None)),
        check_vma=False,
    )
```

profile of v0, /device:TPU:0, one launch (start us, length us, event | category | flops | bytes accessed | tf_op | source)
XLA Modules:
  0.0 570.2 jit_solution(986742737802211337)
XLA Ops:
  9.7 55.3 %all_to_all.57 = bf16[8,64,2048]{2,1,0:T(8,128)(2,1)S(1)} all-to-all(bf16[8,64,2048]{2,1,0:T(8,128)(2,1)S(1)} %convert_element_type.76), channel_id=1, replica_groups=mesh['dp'=4,'mp'=8] {'mp'}, dimensions={0} | all-to-all | bytes 4194304 | tf_op jit(solution)/shard_map/all_to_all | solution.py:53
  71.3 4.8 all-to-all-start.3
  77.4 127.0 %all-to-all-done.3 = bf16[8,64,4096]{2,1,0:T(8,128)(2,1)} async-done(((bf16[8,64,4096]{2,1,0:T(8,128)(2,1)}), bf16[8,64,4096]{2,1,0:T(8,128)(2,1)}, u32[]{:S(2)}, u32[]{:S(2)}) %all-to-all-start.3) | async-done | bytes 4194336 | tf_op jit(solution)/shard_map/all_to_all | solution.py:55
  205.8 3.3 all-to-all-start.2
  209.1 3.8 convert_element_type.82
  215.6 3.6 all-to-all-start.4
  224.9 41.1 %all-to-all-done.4 = bf16[8,64,2048]{2,1,0:T(8,128)(2,1)S(1)} async-done(((bf16[8,64,2048]{2,1,0:T(8,128)(2,1)}), bf16[8,64,2048]{2,1,0:T(8,128)(2,1)S(1)}, u32[]{:S(2)}, u32[]{:S(2)}) %all-to-all-start.4) | async-done | bytes 2097184 | tf_op jit(solution)/shard_map/all_to_all | solution.py:54
  266.0 4.3 all-to-all-start
  276.6 24.6 %all-to-all-done = bf16[8,40,2048]{2,1,0:T(8,128)(2,1)} async-done(((bf16[8,40,2048]{2,1,0:T(8,128)(2,1)}), bf16[8,40,2048]{2,1,0:T(8,128)(2,1)}, u32[]{:S(2)}, u32[]{:S(2)}) %all-to-all-start) | async-done | bytes 1310752 | tf_op jit(solution)/shard_map/all_to_all | solution.py:99
  301.3 5.9 %fusion.72 = f32[320,16,128]{2,0,1:T(8,128)S(1)} fusion(bf16[320,2048,1]{1,0,2:T(8,128)(2,1)} %bitcast.5, bf16[16,128,2048]{2,1,0:T(8,128)(2,1)} %bitcast.168), kind=kOutput, calls=%fused_computation.142 | convolution fusion | flops 2684354560 | bytes 12320768 | tf_op jit(solution)/shard_map/dot_general | solution.py:122
  310.3 15.8 %all-gather.9.cloned.1.call-done = bf16[1,2048,4096]{2,1,0:T(8,128)(2,1)} async-done(((bf16[1,512,4096]{2,1,0:T(8,128)(2,1)}), bf16[1,2048,4096]{2,1,0:T(8,128)(2,1)}) %all-gather.9.cloned.1.call-update) | async-done | bytes 16777232 | tf_op jit(solution)/shard_map/all_gather | solution.py:60
  326.2 23.4 %fusion.32 = f32[1024,4096]{1,0:T(8,128)} fusion(bf16[1024,2048]{1,0:T(8,128)(2,1)} %all-gather.7.cloned.1.call-done, bf16[1,2048,4096]{2,1,0:T(8,128)(2,1)} %all-gather.9.cloned.1.call-done), kind=kOutput, calls=%fused_computation.41 | convolution fusion | flops 17179869184 | bytes 37748736 | tf_op jit(solution)/shard_map/dot_general | solution.py:102
  349.6 4.1 slice_bitcast_fusion
  353.6 4.4 slice_bitcast_fusion.9
  360.0 4.3 subtract_convert_fusion
  375.5 42.7 %while.22 = (s32[]{:T(128)}, bf16[16,160,128]{2,1,0:T(8,128)(2,1)S(1)}, bf16[16,160,128]{2,1,0:T(8,128)(2,1)}, bf16[16,512,128]{2,1,0:T(8,128)(2,1)}, bf16[16,51...) while((s32[]{:T(128)}, ...), condition=%wide.region_9.10_spmd.clone, body=%wide.region_6.9_spmd.clone.sunk | while | flops 42700480 | bytes 1334357 | solution.py:155
  420.2 42.7 %while.23 = (s32[]{:T(128)}, bf16[16,160,128]{2,1,0:T(8,128)(2,1)S(1)}, bf16[16,160,128]{2,1,0:T(8,128)(2,1)}, bf16[16,512,128]{2,1,0:T(8,128)(2,1)}, bf16[16,51...) while((s32[]{:T(128)}, ...), condition=%wide.region_13.14_spmd.clone, body=%wide.region_10.13_spmd.clone.sunk | while | flops 42700480 | bytes 1334357 | solution.py:155
  463.5 7.4 %fusion.36 = bf16[320,2048]{1,0:T(8,128)(2,1)} fusion(bf16[1,2048,2048]{2,1,0:T(8,128)(2,1)} %all-gather.11.cloned.1.call-done, bf16[40,8,16,128]{3,2,1,0:T(8,128)(2,1)S(1)} %bitcast.167), kind=kOutput, calls=%fused_computation.55 | convolution fusion | flops 2685009920 | bytes 11010048 | tf_op jit(solution)/shard_map/dot_general | solution.py:157
  470.9 5.9 %all-to-all-start.5 = ((bf16[8,40,2048]{2,1,0:T(8,128)(2,1)}), bf16[8,40,2048]{2,1,0:T(8,128)(2,1)}, u32[]{:S(2)}, u32[]{:S(2)}) async-start(bf16[8,40,2048]{2,1,0:T(8,128)(2,1)} %bitcast.32), calls=%async_computation.5 | async-start | bytes 2621440 | tf_op jit(solution)/shard_map/all_to_all | solution.py:161
  476.9 4.2 slice.107
  487.7 5.6 copy.35
  493.3 15.4 %all-to-all-done.5 = bf16[8,40,2048]{2,1,0:T(8,128)(2,1)} async-done(((bf16[8,40,2048]{2,1,0:T(8,128)(2,1)}), bf16[8,40,2048]{2,1,0:T(8,128)(2,1)}, u32[]{:S(2)}, u32[]{:S(2)}) %all-to-all-start.5) | async-done | bytes 1310752 | tf_op jit(solution)/shard_map/all_to_all | solution.py:161
  508.7 3.6 all-to-all-start.6
  515.8 45.0 %all-to-all-done.6 = bf16[8,2,16,4096]{3,1,2,0:T(2,128)(2,1)S(1)} async-done(((bf16[8,2,16,4096]{3,1,2,0:T(2,128)(2,1)}), bf16[8,2,16,4096]{3,1,2,0:T(2,128)(2,1)S(1)}, u32[]{:S(2)}, u32[]{:S(2)}) %all-to-all-start.6) | async-done | bytes 2097184 | tf_op jit(solution)/shard_map/all_to_all | solution.py:121
  (186 shorter events, 142.3 us)
Async XLA Ops:
  7.2 505.2 %copy-start = (bf16[2048,8]{0,1:T(8,128)(2,1)S(1)}, bf16[2048,8]{0,1:T(8,128)(2,1)}, u32[]{:S(2)}) copy-start(bf16[2048,8]{0,1:T(8,128)(2,1)} %param.15) | copy-start | bytes 98308
  7.2 294.1 %all-gather.5.cloned.1.call-start = ((), (), s32[]{:S(2)}) async-start(), calls=%async_computation.7 | async-start | bytes 10485760 | tf_op jit(solution)/shard_map/all_gather | solution.py:58
  67.5 1.2 copy-start.6
  71.3 4.8 copy-start.5
  71.3 5.1 copy-start.7
  71.3 133.1 %all-to-all-start.3 = ((bf16[8,64,4096]{2,1,0:T(8,128)(2,1)}), bf16[8,64,4096]{2,1,0:T(8,128)(2,1)}, u32[]{:S(2)}, u32[]{:S(2)}) async-start(bf16[8,64,4096]{2,1,0:T(8,128)(2,1)} %reshape.481), calls=%async_computation.3 | async-start | bytes 8388608 | tf_op jit(solution)/shard_map/all_to_all | solution.py:55
  76.1 234.3 %all-gather.7.cloned.1.call-start = ((), (), s32[]{:S(2)}) async-start(), calls=%async_computation.8 | async-start | bytes 4718592 | tf_op jit(solution)/shard_map/all_gather | solution.py:101
  77.3 127.1 %copy-start.9 = (s32[128,2]{0,1:T(2,128)S(1)}, s32[128,2]{0,1:T(2,128)}, u32[]{:S(2)}) copy-start(s32[128,2]{0,1:T(2,128)} %param.16) | copy-start | bytes 3076
  77.3 248.8 %all-gather.9.cloned.1.call-start = ((), (), s32[]{:S(2)}) async-start(), calls=%async_computation.9 | async-start | bytes 20971520 | tf_op jit(solution)/shard_map/all_gather | solution.py:60
  205.8 9.8 %all-to-all-start.2 = ((s32[8,1,40]{2,1,0:T(1,128)}), s32[8,1,40]{2,1,0:T(1,128)S(1)}, u32[]{:S(2)}, u32[]{:S(2)}) async-start(s32[8,1,40]{2,1,0:T(1,128)} %bitcast.12), calls=%async_computation.2 | async-start | bytes 8192 | tf_op jit(solution)/shard_map/all_to_all | solution.py:100
  212.9 6.4 %copy-start.1 = (bf16[128,2048]{1,0:T(8,128)(2,1)S(1)}, bf16[128,2048]{1,0:T(8,128)(2,1)}, u32[]{:S(2)}) copy-start(bf16[128,2048]{1,0:T(8,128)(2,1)} %fusion.46) | copy-start | bytes 1572868
  215.6 50.4 %all-to-all-start.4 = ((bf16[8,64,2048]{2,1,0:T(8,128)(2,1)}), bf16[8,64,2048]{2,1,0:T(8,128)(2,1)S(1)}, u32[]{:S(2)}, u32[]{:S(2)}) async-start(bf16[8,64,2048]{2,1,0:T(8,128)(2,1)} %convert_element_type.82), calls=%async_computation.4 | async-start | bytes 4194304 | tf_op jit(solution)/shard_map/all_to_all | solution.py:54
  222.3 48.4 %copy-start.8 = (s32[8]{0:T(128)S(1)}, s32[8]{0:T(128)}, u32[]{:S(2)}) copy-start(s32[8]{0:T(128)} %param.17) | copy-start | bytes 100
  266.0 10.7 %copy-start.4 = (bf16[8,64,2048]{2,1,0:T(8,128)(2,1)}, bf16[8,64,2048]{2,1,0:T(8,128)(2,1)S(1)}, u32[]{:S(2)}) copy-start(bf16[8,64,2048]{2,1,0:T(8,128)(2,1)S(1)} %all-to-all-done.4) | copy-start | bytes 6291460
  266.0 35.3 %all-to-all-start = ((bf16[8,40,2048]{2,1,0:T(8,128)(2,1)}), bf16[8,40,2048]{2,1,0:T(8,128)(2,1)}, u32[]{:S(2)}, u32[]{:S(2)}) async-start(bf16[8,40,2048]{2,1,0:T(8,128)(2,1)} %broadcast_select_fusion), calls=%async_computation | async-start | bytes 2621440 | tf_op jit(solution)/shard_map/all_to_all | solution.py:99
  270.2 193.3 %all-gather.11.cloned.1.call-start = ((), (), s32[]{:S(2)}) async-start(), calls=%async_computation.10 | async-start | bytes 10485760 | tf_op jit(solution)/shard_map/all_gather | solution.py:59
  366.7 1.9 copy-start.2
  470.9 5.9 %copy-start.10 = (s32[1,1,8]{2,1,0:T(1,128)S(1)}, s32[1,1,8]{2,1,0:T(1,128)}, u32[]{:S(2)}) copy-start(s32[1,1,8]{2,1,0:T(1,128)} %param.21) | copy-start | bytes 100
  470.9 37.8 %all-to-all-start.5 = ((bf16[8,40,2048]{2,1,0:T(8,128)(2,1)}), bf16[8,40,2048]{2,1,0:T(8,128)(2,1)}, u32[]{:S(2)}, u32[]{:S(2)}) async-start(bf16[8,40,2048]{2,1,0:T(8,128)(2,1)} %bitcast.32), calls=%async_computation.5 | async-start | bytes 2621440 | tf_op jit(solution)/shard_map/all_to_all | solution.py:161
  476.9 4.6 copy-start.3
  508.7 52.1 %all-to-all-start.6 = ((bf16[8,2,16,4096]{3,1,2,0:T(2,128)(2,1)}), bf16[8,2,16,4096]{3,1,2,0:T(2,128)(2,1)S(1)}, u32[]{:S(2)}, u32[]{:S(2)}) async-start(bf16[8,2,16,4096]{3,1,2,0:T(2,128)(2,1)} %copy.35), calls=%async_computation.6 | async-start | bytes 4194304 | tf_op jit(solution)/shard_map/all_to_all | solution.py:121
Sparse Core Ops, SparseCore 0:
  67.7 57.3 all-gather.4
  127.7 91.9 all-gather.6
  221.3 104.7 all-gather.8
  328.1 58.2 all-gather.10
where the time goes:
time: 576 us; the launch traced here: 570 us
  waiting for transfers between devices  272 us (47%)
  matrix products  119 us (21%)
  blocking collectives  55.3 us (10%)
  local copies, waits for them, and re-layouts  50.5 us (9%)
  other arithmetic  32.3 us (6%)
  starting transfers between devices  26.1 us (5%)
  between operations  14.4 us (2%)
    all_to_all x1, waiting for transfers between devices, on_device(): lax.all_to_all(pair_part, 'mp', split_axis=0, concat_axis=1, tiled=True)  127 us
    all_to_all x1, blocking collectives, on_device(): lax.all_to_all(query_part, 'mp', split_axis=0, concat_axis=1, tiled=True)  55.3 us
    all_to_all x1, waiting for transfers between devices, on_device(): lax.all_to_all(outgoing_pages, 'mp', split_axis=0, concat_axis=0, tiled=T...  45 us
    all_to_all x1, waiting for transfers between devices, on_device(): lax.all_to_all(output_part, 'mp', split_axis=0, concat_axis=1, tiled=True)  41.1 us
    dot_general x32, matrix products, one_head(): lax.dot_general(query_head, key_head, (((1,), (1,)), ((), ())), preferred...  39.8 us
    dot_general x32, matrix products, one_head(): jnp.dot(softened, value_head, preferred_element_type=jnp.float32)  37.8 us
    all_to_all x1, waiting for transfers between devices, on_device(): lax.all_to_all(outgoing, 'mp', split_axis=0, concat_axis=0, tiled=True)  24.6 us
    dot_general x1, matrix products, on_device(): projected = jnp.dot(segment, pair_w, preferred_element_type=jnp.float32)  23.4 us
  transfers between devices with their start and end apart: 10, of which 7 were waited for; matrix products, arithmetic and copies ran while one was open for 32% of the time, Pallas kernels for 0%

commit v1 on v0

--- a/solution.py
+++ b/solution.py
@@ -24,6 +24,26 @@
 def on_device(
     tokens, norm_gain, router, routes, prompt_lengths, wq_train, wo_train, wkv_train, page_table
 ):
+
+    def _register_sides(matrix, array_dim, k_dim):
+        mid_arr = lax.axis_size("mp")
+        reached = lax.axis_index("mp")
+        after, moved = (mid_arr, reached)
+        heard = matrix.shape[array_dim] // after
+        v_now = list(matrix.shape)
+        v_now[array_dim] = heard
+        u1 = v_now[k_dim]
+        v_now[k_dim] = u1 * after
+        odd = jnp.zeros(v_now, matrix.dtype)
+        for s in range(after):
+            new = lax.dynamic_slice_in_dim(matrix, (moved ^ s) * heard, heard, axis=array_dim)
+            if s:
+                r1 = range(after)
+                a_now = map(lambda at: (at, at ^ s), r1)
+                new = lax.ppermute(new, axis_name="mp", perm=list(a_now))
+            odd = lax.dynamic_update_slice_in_dim(odd, new, (moved ^ s) * u1, axis=k_dim)
+        return odd
+
     mp_count = lax.axis_size("mp")
     experts = wq_train.shape[0]
     blocks = mp_count // experts
@@ -118,7 +138,7 @@
         "cq,qpk->cpk", placing, own_pages, preferred_element_type=jnp.float32
     ).astype(jnp.bfloat16)
     outgoing_pages = outgoing_pages.reshape(mp_count, PCAP, PAGE, 2 * block_width)
-    page_pool = lax.all_to_all(outgoing_pages, "mp", split_axis=0, concat_axis=0, tiled=True)
+    page_pool = _register_sides(outgoing_pages, 0, 0)
     queries = jnp.dot(arrived.reshape(-1, model_width), query_w, preferred_element_type=jnp.float32)
     query_places = arrived_places.reshape(-1)
     queries = (

time: 576 us -> 567 us (0.984)
  the two profiles are of different devices: /device:TPU:0 before, /device:TPU:8 now
where the time goes in v1:
time: 567 us; the launch traced here: 559 us
  waiting for transfers between devices  246 us (43%)
  matrix products  119 us (21%)
  local copies, waits for them, and re-layouts  53.9 us (10%)
  blocking collectives  53.4 us (9%)
  starting transfers between devices  41.3 us (7%)
  other arithmetic  30.5 us (5%)
  between operations  14.5 us (3%)
    all_to_all x1, waiting for transfers between devices, on_device(): lax.all_to_all(pair_part, 'mp', split_axis=0, concat_axis=1, tiled=True)  123 us
    all_to_all x1, blocking collectives, on_device(): lax.all_to_all(query_part, 'mp', split_axis=0, concat_axis=1, tiled=True)  53.4 us
    ppermute x7, waiting for transfers between devices, _register_sides(): new = lax.ppermute(new, axis_name='mp', perm=list(a_now))  42.1 us
    dot_general x32, matrix products, one_head(): lax.dot_general(query_head, key_head, (((1,), (1,)), ((), ())), preferred...  39.8 us
    dot_general x32, matrix products, one_head(): jnp.dot(softened, value_head, preferred_element_type=jnp.float32)  37.8 us
    all_to_all x1, waiting for transfers between devices, on_device(): lax.all_to_all(output_part, 'mp', split_axis=0, concat_axis=1, tiled=True)  37.4 us
    dot_general x1, matrix products, on_device(): projected = jnp.dot(segment, pair_w, preferred_element_type=jnp.float32)  23.6 us
    all_to_all x1, waiting for transfers between devices, on_device(): lax.all_to_all(outgoing, 'mp', split_axis=0, concat_axis=0, tiled=True)  22.9 us
  transfers between devices with their start and end apart: 16, of which 7 were waited for; matrix products, arithmetic and copies ran while one was open for 35% of the time, Pallas kernels for 0%

profile of v1, /device:TPU:8, one launch (start us, length us, event | category | flops | bytes accessed | tf_op | source)
XLA Modules:
  0.0 559.3 jit_solution(15432991972636414642)
XLA Ops:
  9.7 53.4 %all_to_all.52 = bf16[8,64,2048]{2,1,0:T(8,128)(2,1)S(1)} all-to-all(bf16[8,64,2048]{2,1,0:T(8,128)(2,1)S(1)} %convert_element_type.76), channel_id=1, replica_groups=mesh['dp'=4,'mp'=8] {'mp'}, dimensions={0} | all-to-all | bytes 4194304 | tf_op jit(solution)/shard_map/all_to_all | solution.py:73
  68.2 5.6 %all-to-all-start.3 = ((bf16[8,64,4096]{2,1,0:T(8,128)(2,1)}), bf16[8,64,4096]{2,1,0:T(8,128)(2,1)}, u32[]{:S(2)}, u32[]{:S(2)}) async-start(bf16[8,64,4096]{2,1,0:T(8,128)(2,1)} %reshape.481), calls=%async_computation.3 | async-start | bytes 8388608 | tf_op jit(solution)/shard_map/all_to_all | solution.py:75
  75.1 123.4 %all-to-all-done.3 = bf16[8,64,4096]{2,1,0:T(8,128)(2,1)} async-done(((bf16[8,64,4096]{2,1,0:T(8,128)(2,1)}), bf16[8,64,4096]{2,1,0:T(8,128)(2,1)}, u32[]{:S(2)}, u32[]{:S(2)}) %all-to-all-start.3) | async-done | bytes 4194336 | tf_op jit(solution)/shard_map/all_to_all | solution.py:75
  199.9 7.0 %all-to-all-start.2 = ((s32[8,1,40]{2,1,0:T(1,128)}), s32[8,1,40]{2,1,0:T(1,128)S(1)}, u32[]{:S(2)}, u32[]{:S(2)}) async-start(s32[8,1,40]{2,1,0:T(1,128)} %bitcast.12), calls=%async_computation.2 | async-start | bytes 8192 | tf_op jit(solution)/shard_map/all_to_all | solution.py:120
  206.8 3.8 convert_element_type.82
  212.0 5.0 all-to-all-start.4
  222.6 37.4 %all-to-all-done.4 = bf16[8,64,2048]{2,1,0:T(8,128)(2,1)S(1)} async-done(((bf16[8,64,2048]{2,1,0:T(8,128)(2,1)}), bf16[8,64,2048]{2,1,0:T(8,128)(2,1)S(1)}, u32[]{:S(2)}, u32[]{:S(2)}) %all-to-all-start.4) | async-done | bytes 2097184 | tf_op jit(solution)/shard_map/all_to_all | solution.py:74
  260.0 7.9 %all-to-all-start = ((bf16[8,40,2048]{2,1,0:T(8,128)(2,1)}), bf16[8,40,2048]{2,1,0:T(8,128)(2,1)}, u32[]{:S(2)}, u32[]{:S(2)}) async-start(bf16[8,40,2048]{2,1,0:T(8,128)(2,1)} %broadcast_select_fusion), calls=%async_computation | async-start | bytes 2621440 | tf_op jit(solution)/shard_map/all_to_all | solution.py:119
  272.9 22.9 %all-to-all-done = bf16[8,40,2048]{2,1,0:T(8,128)(2,1)} async-done(((bf16[8,40,2048]{2,1,0:T(8,128)(2,1)}), bf16[8,40,2048]{2,1,0:T(8,128)(2,1)}, u32[]{:S(2)}, u32[]{:S(2)}) %all-to-all-start) | async-done | bytes 1310752 | tf_op jit(solution)/shard_map/all_to_all | solution.py:119
  295.8 6.0 %fusion.72 = f32[320,16,128]{2,0,1:T(8,128)S(1)} fusion(bf16[320,2048,1]{1,0,2:T(8,128)(2,1)} %bitcast.5, bf16[16,128,2048]{2,1,0:T(8,128)(2,1)} %bitcast.168), kind=kOutput, calls=%fused_computation.158 | convolution fusion | flops 2684354560 | bytes 12320768 | tf_op jit(solution)/shard_map/dot_general | solution.py:142
  305.0 18.4 %all-gather.9.cloned.1.call-done = bf16[1,2048,4096]{2,1,0:T(8,128)(2,1)} async-done(((bf16[1,512,4096]{2,1,0:T(8,128)(2,1)}), bf16[1,2048,4096]{2,1,0:T(8,128)(2,1)}) %all-gather.9.cloned.1.call-update) | async-done | bytes 16777232 | tf_op jit(solution)/shard_map/all_gather | solution.py:80
  323.4 23.6 %fusion.32 = f32[1024,4096]{1,0:T(8,128)} fusion(bf16[1024,2048]{1,0:T(8,128)(2,1)} %all-gather.7.cloned.1.call-done, bf16[1,2048,4096]{2,1,0:T(8,128)(2,1)} %all-gather.9.cloned.1.call-done), kind=kOutput, calls=%fused_computation.41 | convolution fusion | flops 17179869184 | bytes 37748736 | tf_op jit(solution)/shard_map/dot_general | solution.py:122
  347.0 4.1 slice_bitcast_fusion
  351.1 4.0 slice.107
  355.1 6.3 %slice_bitcast_fusion.9 = bf16[128,8,16,128]{3,1,2,0:T(8,128)(2,1)} fusion(f32[1024,4096]{1,0:T(8,128)} %fusion.32), kind=kLoop, calls=%fused_computation.157 | loop fusion | bytes 8388608
  363.4 3.7 subtract_convert_fusion
  375.1 3.3 reshape.489
  378.4 3.2 constant_dynamic-slice_fusion
  397.5 42.7 %while.22 = (s32[]{:T(128)}, bf16[16,160,128]{2,1,0:T(8,128)(2,1)S(1)}, bf16[16,160,128]{2,1,0:T(8,128)(2,1)}, bf16[16,512,128]{2,1,0:T(8,128)(2,1)}, bf16[16,51...) while((s32[]{:T(128)}, ...), condition=%wide.region_9.10_spmd.clone, body=%wide.region_6.9_spmd.clone.sunk | while | flops 42700480 | bytes 1334357 | solution.py:175
  442.1 42.7 %while.23 = (s32[]{:T(128)}, bf16[16,160,128]{2,1,0:T(8,128)(2,1)S(1)}, bf16[16,160,128]{2,1,0:T(8,128)(2,1)}, bf16[16,512,128]{2,1,0:T(8,128)(2,1)}, bf16[16,51...) while((s32[]{:T(128)}, ...), condition=%wide.region_13.14_spmd.clone, body=%wide.region_10.13_spmd.clone.sunk | while | flops 42700480 | bytes 1334357 | solution.py:175
  485.5 7.4 %fusion.36 = bf16[320,2048]{1,0:T(8,128)(2,1)} fusion(bf16[1,2048,2048]{2,1,0:T(8,128)(2,1)} %all-gather.11.cloned.1.call-done, bf16[40,8,16,128]{3,2,1,0:T(8,128)(2,1)S(1)} %bitcast.167), kind=kOutput, calls=%fused_computation.55 | convolution fusion | flops 2685009920 | bytes 11010048 | tf_op jit(solution)/shard_map/dot_general | solution.py:177
  492.9 5.4 all-to-all-start.5
  508.3 38.1 %collective-permute-done.5 = bf16[1,2,16,4096]{3,1,0,2:T(2,128)(2,1)S(1)} collective-permute-done((bf16[1,2,16,4096]{3,1,0,2:T(2,128)(2,1)S(1)}, bf16[1,2,16,4096]{3,1,0,2:T(2,128)(2,1)S(1)}, u32[]{:S(2)}, u32[]{:S(2)}) %collective-permute-start.5) | collective-permute-done | bytes 262176 | tf_op jit(solution)/shard_map/ppermute | solution.py:43
  546.6 3.9 collective-permute-done.6
  (216 shorter events, 150.2 us)
Async XLA Ops:
  7.2 262.6 %copy-start = (bf16[2048,8]{0,1:T(8,128)(2,1)S(1)}, bf16[2048,8]{0,1:T(8,128)(2,1)}, u32[]{:S(2)}) copy-start(bf16[2048,8]{0,1:T(8,128)(2,1)} %param.15) | copy-start | bytes 98308
  7.2 288.6 %all-gather.5.cloned.1.call-start = ((), (), s32[]{:S(2)}) async-start(), calls=%async_computation.6 | async-start | bytes 10485760 | tf_op jit(solution)/shard_map/all_gather | solution.py:78
  68.2 130.3 %all-to-all-start.3 = ((bf16[8,64,4096]{2,1,0:T(8,128)(2,1)}), bf16[8,64,4096]{2,1,0:T(8,128)(2,1)}, u32[]{:S(2)}, u32[]{:S(2)}) async-start(bf16[8,64,4096]{2,1,0:T(8,128)(2,1)} %reshape.481), calls=%async_computation.3 | async-start | bytes 8388608 | tf_op jit(solution)/shard_map/all_to_all | solution.py:75
  73.8 231.2 %all-gather.7.cloned.1.call-start = ((), (), s32[]{:S(2)}) async-start(), calls=%async_computation.7 | async-start | bytes 4718592 | tf_op jit(solution)/shard_map/all_gather | solution.py:121
  75.0 123.5 %copy-start.14 = (s32[128,2]{0,1:T(2,128)S(1)}, s32[128,2]{0,1:T(2,128)}, u32[]{:S(2)}) copy-start(s32[128,2]{0,1:T(2,128)} %param.16) | copy-start | bytes 3076
  75.0 248.4 %all-gather.9.cloned.1.call-start = ((), (), s32[]{:S(2)}) async-start(), calls=%async_computation.8 | async-start | bytes 20971520 | tf_op jit(solution)/shard_map/all_gather | solution.py:80
  199.9 12.1 %all-to-all-start.2 = ((s32[8,1,40]{2,1,0:T(1,128)}), s32[8,1,40]{2,1,0:T(1,128)S(1)}, u32[]{:S(2)}, u32[]{:S(2)}) async-start(s32[8,1,40]{2,1,0:T(1,128)} %bitcast.12), calls=%async_computation.2 | async-start | bytes 8192 | tf_op jit(solution)/shard_map/all_to_all | solution.py:120
  210.7 6.4 %copy-start.2 = (bf16[128,2048]{1,0:T(8,128)(2,1)S(1)}, bf16[128,2048]{1,0:T(8,128)(2,1)}, u32[]{:S(2)}) copy-start(bf16[128,2048]{1,0:T(8,128)(2,1)} %fusion.46) | copy-start | bytes 1572868
  212.0 48.1 %all-to-all-start.4 = ((bf16[8,64,2048]{2,1,0:T(8,128)(2,1)}), bf16[8,64,2048]{2,1,0:T(8,128)(2,1)S(1)}, u32[]{:S(2)}, u32[]{:S(2)}) async-start(bf16[8,64,2048]{2,1,0:T(8,128)(2,1)} %convert_element_type.82), calls=%async_computation.4 | async-start | bytes 4194304 | tf_op jit(solution)/shard_map/all_to_all | solution.py:74
  220.1 47.8 %copy-start.13 = (s32[8]{0:T(128)S(1)}, s32[8]{0:T(128)}, u32[]{:S(2)}) copy-start(s32[8]{0:T(128)} %param.17) | copy-start | bytes 100
  220.1 49.9 %copy-start.15 = (s32[1,1,8]{2,1,0:T(1,128)S(1)}, s32[1,1,8]{2,1,0:T(1,128)}, u32[]{:S(2)}) copy-start(s32[1,1,8]{2,1,0:T(1,128)} %param.21) | copy-start | bytes 100
  260.0 12.9 %copy-start.6 = (bf16[8,64,2048]{2,1,0:T(8,128)(2,1)}, bf16[8,64,2048]{2,1,0:T(8,128)(2,1)S(1)}, u32[]{:S(2)}) copy-start(bf16[8,64,2048]{2,1,0:T(8,128)(2,1)S(1)} %all-to-all-done.4) | copy-start | bytes 6291460
  260.0 35.8 %all-to-all-start = ((bf16[8,40,2048]{2,1,0:T(8,128)(2,1)}), bf16[8,40,2048]{2,1,0:T(8,128)(2,1)}, u32[]{:S(2)}, u32[]{:S(2)}) async-start(bf16[8,40,2048]{2,1,0:T(8,128)(2,1)} %broadcast_select_fusion), calls=%async_computation | async-start | bytes 2621440 | tf_op jit(solution)/shard_map/all_to_all | solution.py:119
  267.9 217.7 %all-gather.11.cloned.1.call-start = ((), (), s32[]{:S(2)}) async-start(), calls=%async_computation.9 | async-start | bytes 10485760 | tf_op jit(solution)/shard_map/all_gather | solution.py:79
  378.4 10.5 %copy-start.4 = (bf16[1024,16,128]{2,1,0:T(8,128)(2,1)S(1)}, bf16[1024,16,128]{2,1,0:T(8,128)(2,1)}, u32[]{:S(2)}) copy-start(bf16[1024,16,128]{2,1,0:T(8,128)(2,1)} %copy-done.3) | copy-start | bytes 12582916
  381.7 118.0 %collective-permute-start = (bf16[1,2,16,4096]{3,1,0,2:T(2,128)(2,1)}, bf16[1,2,16,4096]{3,1,0,2:T(2,128)(2,1)}, u32[]{:S(2)}, u32[]{:S(2)}) collective-permute-start(bf16[1,2,16,4096]{3,1,0,2:T(2,128)(2,1)} %get-tuple-element.196), channel_id=1, source_target_pairs={{0,1},{1,0},{2,3},{3,2},{4,5},{5,4},{6,7},{7,6},{8,9},{9,8},{10,11... | collective-permute-start | bytes 786440 | tf_op jit(solution)/shard_map/ppermute | solution.py:43
  383.1 119.2 %collective-permute-start.1 = (bf16[1,2,16,4096]{3,1,0,2:T(2,128)(2,1)}, bf16[1,2,16,4096]{3,1,0,2:T(2,128)(2,1)}, u32[]{:S(2)}, u32[]{:S(2)}) collective-permute-start(bf16[1,2,16,4096]{3,1,0,2:T(2,128)(2,1)} %get-tuple-element.195), channel_id=1, source_target_pairs={{0,2},{1,3},{2,0},{3,1},{4,6},{5,7},{6,4},{7,5},{8,10},{9,11},{10,... | collective-permute-start | bytes 786440 | tf_op jit(solution)/shard_map/ppermute | solution.py:43
  383.6 121.3 %collective-permute-start.2 = (bf16[1,2,16,4096]{3,1,0,2:T(2,128)(2,1)}, bf16[1,2,16,4096]{3,1,0,2:T(2,128)(2,1)}, u32[]{:S(2)}, u32[]{:S(2)}) collective-permute-start(bf16[1,2,16,4096]{3,1,0,2:T(2,128)(2,1)} %get-tuple-element.194), channel_id=1, source_target_pairs={{0,3},{1,2},{2,1},{3,0},{4,7},{5,6},{6,5},{7,4},{8,11},{9,10},{10,... | collective-permute-start | bytes 786440 | tf_op jit(solution)/shard_map/ppermute | solution.py:43
  385.2 120.9 %collective-permute-start.3 = (bf16[1,2,16,4096]{3,1,0,2:T(2,128)(2,1)}, bf16[1,2,16,4096]{3,1,0,2:T(2,128)(2,1)}, u32[]{:S(2)}, u32[]{:S(2)}) collective-permute-start(bf16[1,2,16,4096]{3,1,0,2:T(2,128)(2,1)} %get-tuple-element.193), channel_id=1, source_target_pairs={{0,4},{1,5},{2,6},{3,7},{4,0},{5,1},{6,2},{7,3},{8,12},{9,13},{10,... | collective-permute-start | bytes 786440 | tf_op jit(solution)/shard_map/ppermute | solution.py:43
  387.6 119.7 %collective-permute-start.4 = (bf16[1,2,16,4096]{3,1,0,2:T(2,128)(2,1)}, bf16[1,2,16,4096]{3,1,0,2:T(2,128)(2,1)}, u32[]{:S(2)}, u32[]{:S(2)}) collective-permute-start(bf16[1,2,16,4096]{3,1,0,2:T(2,128)(2,1)} %get-tuple-element.192), channel_id=1, source_target_pairs={{0,5},{1,4},{2,7},{3,6},{4,1},{5,0},{6,3},{7,2},{8,13},{9,12},{10,... | collective-permute-start | bytes 786440 | tf_op jit(solution)/shard_map/ppermute | solution.py:43
  492.9 57.8 %all-to-all-start.5 = ((bf16[8,40,2048]{2,1,0:T(8,128)(2,1)}), bf16[8,40,2048]{2,1,0:T(8,128)(2,1)S(1)}, u32[]{:S(2)}, u32[]{:S(2)}) async-start(bf16[8,40,2048]{2,1,0:T(8,128)(2,1)} %bitcast.32), calls=%async_computation.5 | async-start | bytes 2621440 | tf_op jit(solution)/shard_map/all_to_all | solution.py:181
  499.7 46.8 %collective-permute-start.5 = (bf16[1,2,16,4096]{3,1,0,2:T(2,128)(2,1)S(1)}, bf16[1,2,16,4096]{3,1,0,2:T(2,128)(2,1)S(1)}, u32[]{:S(2)}, u32[]{:S(2)}) collective-permute-start(bf16[1,2,16,4096]{3,1,0,2:T(2,128)(2,1)S(1)} %copy-done.11), channel_id=1, source_target_pairs={{0,6},{1,7},{2,4},{3,5},{4,2},{5,3},{6,0},{7,1},{8,14},{9,15},{10,... | collective-permute-start | bytes 786440 | tf_op jit(solution)/shard_map/ppermute | solution.py:43
  501.2 51.3 %copy-start.1 = (bf16[2048,8]{0,1:T(8,128)(2,1)S(1)}, bf16[2048,8]{0,1:T(8,128)(2,1)}, u32[]{:S(2)}) copy-start(bf16[2048,8]{0,1:T(8,128)(2,1)} %param.15) | copy-start | bytes 98308
  502.4 48.2 %collective-permute-start.6 = (bf16[1,2,16,4096]{3,1,0,2:T(2,128)(2,1)S(1)}, bf16[1,2,16,4096]{3,1,0,2:T(2,128)(2,1)S(1)}, u32[]{:S(2)}, u32[]{:S(2)}) collective-permute-start(bf16[1,2,16,4096]{3,1,0,2:T(2,128)(2,1)S(1)} %copy-done.10), channel_id=1, source_target_pairs={{0,7},{1,6},{2,5},{3,4},{4,3},{5,2},{6,1},{7,0},{8,15},{9,14},{10,... | collective-permute-start | bytes 786440 | tf_op jit(solution)/shard_map/ppermute | solution.py:43
  (8 other events, 26.9 us)
Sparse Core Ops, SparseCore 0:
  65.7 57.6 all-gather.4
  126.2 88.3 all-gather.6
  216.2 107.2 all-gather.8
  325.4 58.2 all-gather.10
